TPU v7x, 512 devices: a whole 4x8x8 slice. The times are simulated.
512 devices in a mesh: ctx: 32 (over x_hi, y, core), dp: 16 (over x_lo, z).
Axes of the slice: x: 4 (x_hi: 2, x_lo: 2; x = x_hi * 2 + x_lo), y: 8, z: 8, core: 2. Of those that a mesh axis runs over, the one named last changes fastest.
Arguments:
- out_grad: bfloat16 [16, 4096, 256], P('dp', 'ctx'), may hold values from -0.0234375 to 0.0234375
- gate_out: bfloat16 [16, 4096, 256], P('dp', 'ctx'), may hold values from -6 to 6
- gate_in: bfloat16 [16, 4096, 256], P('dp', 'ctx'), may hold values from -6 to 6
- values: bfloat16 [16, 4096, 256], P('dp', 'ctx'), may hold values from -6 to 6
- doc_tiles: int32 [16, 4], P('dp'), may hold values from 0 to 32, as said below
Outputs:
- kernel_derivative: float32 [4096, 256], P('ctx')
Inputs may be any that keep to these rules, and one draw needn't show every extreme that they name: `doc_tiles`: row w lists, in order, the lengths in tiles of the documents of window w; they sum to 32; an entry of 0 stands for no document.
All inputs are finite; a program needn't handle non-finite values.
Results may differ from a plain program's by a relative error of at most 0.0029.
Values may be sent and summed in bfloat16 or wider, within the bound.
A program may use at most 64 MiB of HBM per device.

v0:
```python
import math

import jax
import jax.numpy as jnp
from jax import lax
from jax.sharding import PartitionSpec as P

tile_width = 128


def precise_matrix_product(matrix, operand):
    return jnp.dot(
        matrix, operand, precision=lax.Precision.HIGHEST, preferred_element_type=jnp.float32
    )


def block_sequence_labels(lengths, tile_count):
    doc_ends = jnp.cumsum(lengths)
    tile_index = jnp.arange(tile_count, dtype=jnp.int32)
    return jnp.sum((tile_index[:, None] >= doc_ends[None, :]).astype(jnp.int32), axis=1)


def transform_tables(lines_each_device_slice):
    repeat_length_span = 2 * lines_each_device_slice
    spectral_bins = jnp.arange(lines_each_device_slice + 1, dtype=jnp.int32)
    sample_positions = jnp.arange(lines_each_device_slice, dtype=jnp.int32)
    rotation_radians = spectral_bins[:, None] * sample_positions[None, :] % repeat_length_span
    angles = rotation_radians.astype(jnp.float32) * (2.0 * math.pi / repeat_length_span)
    forward = jnp.concatenate([jnp.cos(angles), -jnp.sin(angles)], axis=0)
    lag_index = jnp.arange(repeat_length_span, dtype=jnp.int32)
    back_phases = lag_index[:, None] * spectral_bins[None, :] % repeat_length_span
    back_angles = back_phases.astype(jnp.float32) * (2.0 * math.pi / repeat_length_span)
    factor = (
        jnp.where(
            (spectral_bins == 0) | (spectral_bins == lines_each_device_slice), 1.0, 2.0
        ).astype(jnp.float32)
        / repeat_length_span
    )
    inverse = jnp.concatenate(
        [jnp.cos(back_angles) * factor[None, :], -jnp.sin(back_angles) * factor[None, :]], axis=1
    )
    return (forward, inverse)


def correlate(forward, inverse, head_hat, source):
    halfway = forward.shape[0] // 2
    source_hat = precise_matrix_product(forward, source)
    head_real, head_imag = (head_hat[:halfway], head_hat[halfway:])
    tail_real, tail_imag = (source_hat[:halfway], source_hat[halfway:])
    product = jnp.concatenate(
        [
            head_real * tail_real + head_imag * tail_imag,
            head_imag * tail_real - head_real * tail_imag,
        ],
        axis=0,
    )
    return precise_matrix_product(inverse, product)


def add_block(incomplete_total, addend, block_index):
    current = lax.dynamic_index_in_dim(incomplete_total, block_index, 0, keepdims=False)
    return lax.dynamic_update_index_in_dim(incomplete_total, current + addend, block_index, 0)


def own_lags(forward, inverse, weighted, gated_own, own_tiles):
    lines_each_device_slice = weighted.shape[0]
    own_doc = jnp.repeat(own_tiles, tile_width)
    doc_mask = (own_doc == own_tiles[0]).astype(jnp.float32)[:, None]
    segment_hat = precise_matrix_product(forward, weighted * doc_mask)
    starts = jnp.float32(1.0)
    inside = correlate(forward, inverse, segment_hat, gated_own * doc_mask)
    lags = inside[:lines_each_device_slice] * starts
    return (lags, segment_hat)


def per_device(out_grad, gate_out, gate_in, values, doc_tiles):
    lines_each_device_slice = out_grad.shape[1]
    channels = out_grad.shape[2]
    shards = lax.axis_size("ctx")
    own_index = lax.axis_index("ctx")
    per_shard = lines_each_device_slice // tile_width
    weighted = gate_out[0].astype(jnp.float32) * out_grad[0].astype(jnp.float32)
    gated_input = (gate_in[0].astype(jnp.float32) * values[0].astype(jnp.float32)).astype(
        jnp.bfloat16
    )
    tile_doc = block_sequence_labels(doc_tiles[0], shards * per_shard)
    own_tiles = lax.dynamic_slice_in_dim(tile_doc, own_index * per_shard, per_shard)
    head_doc = own_tiles[0]
    forward, inverse = transform_tables(lines_each_device_slice)
    gated_own = gated_input.astype(jnp.float32)
    inside_lags, head_hat = own_lags(forward, inverse, weighted, gated_own, own_tiles)
    incomplete_total = (
        jnp.zeros((shards, lines_each_device_slice, channels), jnp.float32).at[0].set(inside_lags)
    )
    piece = lax.all_gather(gated_input, "ctx", axis=0, tiled=True)
    pieces_in = piece.shape[0] // lines_each_device_slice

    def one_source(member, carried):
        source = lax.dynamic_slice_in_dim(
            piece, member * lines_each_device_slice, lines_each_device_slice, 0
        ).astype(jnp.float32)
        source_tiles = lax.dynamic_slice_in_dim(tile_doc, member * per_shard, per_shard)
        tail_doc = source_tiles[per_shard - 1]
        doc_mask = (jnp.repeat(source_tiles, tile_width) == tail_doc).astype(jnp.float32)[:, None]
        usable = (member < own_index) & (tail_doc == head_doc)
        lag_block = jnp.clip(own_index - member, 1, shards - 1)
        lag_terms = correlate(forward, inverse, head_hat, source * doc_mask) * usable.astype(
            jnp.float32
        )
        carried = add_block(carried, lag_terms[:lines_each_device_slice], lag_block)
        return add_block(carried, lag_terms[lines_each_device_slice:], lag_block - 1)

    incomplete_total = lax.fori_loop(0, pieces_in, one_source, incomplete_total)
    stacked_rows = incomplete_total.reshape(shards * lines_each_device_slice, channels)
    owned = lax.psum_scatter(stacked_rows, "ctx", scatter_dimension=0, tiled=True)
    return lax.psum(owned, "dp")


def solution(mesh):
    in_specs = (
        P("dp", "ctx", None),
        P("dp", "ctx", None),
        P("dp", "ctx", None),
        P("dp", "ctx", None),
        P("dp", None),
    )
    out_specs = P("ctx", None)
    return jax.shard_map(
        per_device, mesh=mesh, in_specs=in_specs, out_specs=out_specs, check_vma=False
    )
```

profile of v0, /device:TPU:56, one launch (start us, length us, event | category | flops | bytes accessed | tf_op | source)
XLA Modules:
  0.0 611.2 jit_solution(9955731453614005366)
XLA Ops:
  6.5 1.5 multiply_convert_fusion
  10.1 1.1 fusion.33
  11.2 1.2 fusion.22
  13.3 2.4 scatter.4.clone
  16.4 82.5 %all-gather.3.cloned.1.call-done = bf16[1,4096,256]{2,1,0:T(8,128)(2,1)} async-done(((bf16[1,128,256]{2,1,0:T(8,128)(2,1)}), bf16[1,4096,256]{2,1,0:T(8,128)(2,1)}) %all-gather.3.cloned.1.call-update) | async-done | bytes 2097168 | tf_op jit(solution)/shard_map/all_gather | solution.py:95
  98.9 223.2 %while.18 = (s32[]{:T(128)}, f32[32,128,256]{1,2,0:T(8,128)}, s32[]{:T(128)}, f32[258,256]{1,0:T(8,128)S(1)}, bf16[4096,256]{1,0:T(8,128)(2,1)}, /*index=5*/f32[...) while((s32[]{:T(128)}, f32[32,128,256]{1,2,0:T(8,128)}, ...), condition=%wide.region_3.4_spmd, body=%wide.region_2.3_spmd.sunk | while | flops 304744448 | bytes 3355979 | solution.py:113
  98.9 1.1 convolution_bitcast_fusion.3
  105.9 1.1 convolution_bitcast_fusion.3
  126.8 1.1 convolution_bitcast_fusion.3
  140.8 1.1 convolution_bitcast_fusion.3
  147.8 1.1 convolution_bitcast_fusion.3
  154.8 1.1 convolution_bitcast_fusion.3
  168.7 1.1 convolution_bitcast_fusion.3
  175.7 1.1 convolution_bitcast_fusion.3
  182.7 1.1 convolution_bitcast_fusion.3
  189.7 1.1 convolution_bitcast_fusion.3
  196.7 1.1 convolution_bitcast_fusion.3
  203.6 1.1 convolution_bitcast_fusion.3
  210.6 1.1 convolution_bitcast_fusion.3
  217.6 1.1 convolution_bitcast_fusion.3
  231.5 1.1 convolution_bitcast_fusion.3
  245.5 1.1 convolution_bitcast_fusion.3
  252.4 1.1 convolution_bitcast_fusion.3
  266.4 1.1 convolution_bitcast_fusion.3
  280.3 1.1 convolution_bitcast_fusion.3
  287.3 1.1 convolution_bitcast_fusion.3
  301.2 1.1 convolution_bitcast_fusion.3
  315.2 1.1 convolution_bitcast_fusion.3
  322.1 5.6 copy.12
  327.8 133.0 %reduce-scatter.2.cloned.1.call-done = f32[128,256]{1,0:T(8,128)} async-done(((f32[4096,256]{1,0:T(8,128)}), f32[128,256]{1,0:T(8,128)}) %reduce-scatter.2.cloned.1.call-update) | async-done | bytes 131088 | tf_op jit(solution)/shard_map/reduce_scatter | solution.py:115
  460.9 142.2 %all-reduce.3.cloned.1.call-done = f32[128,256]{1,0:T(8,128)} async-done(((f32[128,256]{1,0:T(8,128)}), f32[128,256]{1,0:T(8,128)}) %all-reduce.3.cloned.1.call-update) | async-done | bytes 131088 | tf_op jit(solution)/shard_map/psum | solution.py:116
  603.1 1.6 copy.23
  (251 shorter events, 162.3 us)
Async XLA Ops:
  6.5 92.4 %all-gather.3.cloned.1.call-start = ((), (), s32[]{:S(2)}) async-start(), calls=%async_computation.3 | async-start | bytes 2162688 | tf_op jit(solution)/shard_map/all_gather | solution.py:95
  8.1 452.8 %reduce-scatter.2.cloned.1.call-start = ((), (), s32[]{:S(2)}) async-start(), calls=%async_computation.1 | async-start | bytes 4325376 | tf_op jit(solution)/shard_map/reduce_scatter | solution.py:115
  327.8 275.3 %all-reduce.3.cloned.1.call-start = ((), (), s32[]{:S(2)}) async-start(), calls=%async_computation.2 | async-start | bytes 262144 | tf_op jit(solution)/shard_map/psum | solution.py:116
Sparse Core Ops, SparseCore 0:
  10.7 88.1 all-gather.2
  327.9 132.9 reduce-scatter.1
  464.0 139.0 all-reduce.2
where the time goes:
time: 615 us; the launch traced here: 611 us
  waiting for transfers between devices  358 us (58%)
  local copies, waits for them, and re-layouts  87.7 us (14%)
  matrix products  64 us (10%)
  other arithmetic  47.8 us (8%)
  loops' own time  40.5 us (7%)
  between operations  13.2 us (2%)
    psum x1, waiting for transfers between devices, per_device(): return lax.psum(owned, 'dp')  142 us
    reduce_scatter x1, waiting for transfers between devices, per_device(): lax.psum_scatter(stacked_rows, 'ctx', scatter_dimension=0, tiled=True)  133 us
    all_gather x1, waiting for transfers between devices, per_device(): piece = lax.all_gather(gated_input, 'ctx', axis=0, tiled=True)  82.5 us
    dot_general x67, matrix products, precise_matrix_product(): jnp.dot(matrix, operand, precision=lax.Precision.HIGHEST, preferred_eleme...  64 us
    dynamic_slice x64, local copies, waits for them, and re-layouts, add_block(): lax.dynamic_index_in_dim(incomplete_total, block_index, 0, keepdims=False)  58.6 us
    dynamic_update_slice x64, other arithmetic, add_block(): lax.dynamic_update_index_in_dim(incomplete_total, current + addend, block...  42.8 us
    another operation x1, loops' own time, per_device(): incomplete_total = lax.fori_loop(0, pieces_in, one_source, incomplete_total)  40.5 us
    dynamic_slice x32, local copies, waits for them, and re-layouts, one_source(): lax.dynamic_slice_in_dim(tile_doc, member * per_shard, per_shard)  18.8 us
  transfers between devices with their start and end apart: 3, of which 3 were waited for; matrix products, arithmetic and copies ran while one was open for 1% of the time, Pallas kernels for 0%

commit v1 on v0

v1 whole, which is shorter than its diff:
```python
import functools

import jax
import jax.numpy as jnp
import numpy as np
from jax import lax
from jax.experimental import pallas as pl
from jax.experimental.pallas import tpu as pltpu
from jax.sharding import PartitionSpec as P

TILE = 128
ROWS = 8
MESH = pl.DeviceIdType.MESH


def transform_tables():
    positions = np.arange(TILE)
    theta = 2.0 * np.pi * (np.arange(TILE) + 0.5) / (2 * TILE)
    forward = np.concatenate(
        [np.cos(positions[:, None] * theta), -np.sin(positions[:, None] * theta)], axis=1
    )
    inverse = np.concatenate(
        [np.cos(theta[:, None] * positions), -np.sin(theta[:, None] * positions)], axis=0
    )
    inverse = inverse / TILE
    pair = []
    for table in (forward, inverse):
        table = table.astype(np.float32)
        high = table.astype(jnp.bfloat16)
        low = (table - high.astype(np.float32)).astype(jnp.bfloat16)
        pair.append(np.stack([high, low]))
    return pair


def product(left, right):
    return jnp.dot(left, right, preferred_element_type=jnp.float32)


def kernel(
    members, windows, out_grad, gate_out, gate_in, values, doc_tiles, forward, inverse, out,
    outgoing, incoming, docs, spectra, sums, lags, parts, total, landing,
    send_sems, recv_sems,
):
    me = lax.axis_index("ctx")
    window = lax.axis_index("dp")
    per_owner = members // windows
    channels = members * ROWS

    barrier = pltpu.get_barrier_semaphore()
    for step in range(1, members):
        pl.semaphore_signal(
            barrier, 1, device_id={"ctx": lax.rem(me + step, members)}, device_id_type=MESH
        )
    for step in range(1, windows):
        pl.semaphore_signal(
            barrier, 1, device_id={"dp": lax.rem(window + step, windows)}, device_id_type=MESH
        )

    with jax.named_scope("gate"):
        weighted = gate_out[0].astype(jnp.float32) * out_grad[0].astype(jnp.float32)
        gated = gate_in[0].astype(jnp.float32) * values[0].astype(jnp.float32)
        weighted = weighted.T.reshape(members, 1, ROWS, TILE)
        gated = gated.T.reshape(members, 1, ROWS, TILE)
        outgoing[...] = (
            jnp.concatenate([weighted, gated], axis=1)
            .reshape(members, 2 * ROWS, TILE)
            .astype(jnp.bfloat16)
        )
        incoming[me] = outgoing[me]

        tile = lax.broadcasted_iota(jnp.int32, docs.shape, 0)
        label = jnp.zeros(docs.shape, jnp.float32)
        end = jnp.int32(0)
        for entry in range(doc_tiles.shape[1]):
            end = end + doc_tiles[0, entry]
            label += (tile >= end).astype(jnp.float32)
        docs[...] = label

    with jax.named_scope("enter"):
        pl.semaphore_wait(barrier, members + windows - 2)

    with jax.named_scope("send_tiles"):
        for step in range(1, members):
            peer = lax.rem(me + step, members)
            pltpu.make_async_remote_copy(
                src_ref=outgoing.at[peer],
                dst_ref=incoming.at[me],
                send_sem=send_sems.at[0],
                recv_sem=recv_sems.at[0],
                device_id={"ctx": peer},
                device_id_type=MESH,
            ).start()
        others = pl.ds(0, members - 1)
        pltpu.make_async_copy(outgoing.at[others], outgoing.at[others], send_sems.at[0]).wait()
        pltpu.make_async_copy(incoming.at[others], incoming.at[others], recv_sems.at[0]).wait()

    with jax.named_scope("transform"):
        tiles = incoming[...].reshape(members * 2 * ROWS, TILE)
        hats = product(tiles, forward[0]) + product(tiles, forward[1])
        spectra[pl.ds(0, members)] = hats.reshape(members, 2 * ROWS, 2 * TILE)
        spectra[pl.ds(members, ROWS)] = jnp.zeros((ROWS, 2 * ROWS, 2 * TILE), jnp.float32)

    with jax.named_scope("pairs"):
        for first in range(0, members, ROWS):

            def lag_block(offset, carried, first=first):
                lag = first + offset
                real = jnp.zeros((ROWS, TILE), jnp.float32)
                imag = jnp.zeros((ROWS, TILE), jnp.float32)
                for source in range(members - first):
                    head = source + lag
                    head_real = spectra[head, :ROWS, :TILE]
                    head_imag = spectra[head, :ROWS, TILE:]
                    tail_real = spectra[source, ROWS:, :TILE]
                    tail_imag = spectra[source, ROWS:, TILE:]
                    same = docs[head] == docs[source]
                    real += jnp.where(same, head_real * tail_real + head_imag * tail_imag, 0.0)
                    imag += jnp.where(same, head_imag * tail_real - head_real * tail_imag, 0.0)
                sums[lag, :, :TILE] = real
                sums[lag, :, TILE:] = imag
                return carried

            lax.fori_loop(0, min(ROWS, members - first), lag_block, 0)
        sums[members] = jnp.zeros((ROWS, 2 * TILE), jnp.float32)

    with jax.named_scope("back"):
        here = sums[pl.ds(0, members)].reshape(members * ROWS, 2 * TILE)
        after = sums[pl.ds(1, members)].reshape(members * ROWS, 2 * TILE)
        parity = lax.broadcasted_iota(jnp.int32, (members * ROWS, TILE), 1) % 2
        sign = (1 - 2 * parity).astype(jnp.float32)
        both = jnp.concatenate(
            [here[:, :TILE] + sign * after[:, TILE:], here[:, TILE:] - sign * after[:, :TILE]], axis=1
        )
        high = both.astype(jnp.bfloat16)
        low = (both - high.astype(jnp.float32)).astype(jnp.bfloat16)
        result = product(high, inverse[0]) + product(low, inverse[0]) + product(high, inverse[1])
        lags[...] = result.reshape(lags.shape).astype(lags.dtype)
        parts[window] = lags[window]

    with jax.named_scope("send_lags"):
        for step in range(1, windows):
            peer = lax.rem(window + step, windows)
            pltpu.make_async_remote_copy(
                src_ref=lags.at[peer],
                dst_ref=parts.at[window],
                send_sem=send_sems.at[1],
                recv_sem=recv_sems.at[1],
                device_id={"dp": peer},
                device_id_type=MESH,
            ).start()
        others = pl.ds(0, windows - 1)
        pltpu.make_async_copy(lags.at[others], lags.at[others], send_sems.at[1]).wait()
        pltpu.make_async_copy(parts.at[others], parts.at[others], recv_sems.at[1]).wait()
        total[...] = jnp.sum(parts[...].astype(jnp.float32), axis=0).reshape(total.shape)

    with jax.named_scope("spread"):
        for step in range(windows):
            reader = lax.rem(window + step, windows)
            for block in range(per_owner):
                lag = window * per_owner + block
                own = (reader == window) & (lag == me)

                @pl.when(own)
                def _():
                    pltpu.make_async_copy(total.at[block], landing.at[me], recv_sems.at[2]).start()

                @pl.when(jnp.logical_not(own))
                def _():
                    pltpu.make_async_remote_copy(
                        src_ref=total.at[block],
                        dst_ref=landing.at[me],
                        send_sem=send_sems.at[2],
                        recv_sem=recv_sems.at[2],
                        device_id={"ctx": lag, "dp": reader},
                        device_id_type=MESH,
                    ).start()

        keeps = me // per_owner == window
        count = windows * per_owner
        span = landing.at[pl.ds(0, count)]
        fewer = landing.at[pl.ds(0, count - 1)]

        @pl.when(keeps)
        def _():
            pltpu.make_async_copy(fewer, fewer, send_sems.at[2]).wait()

        @pl.when(jnp.logical_not(keeps))
        def _():
            pltpu.make_async_copy(span, span, send_sems.at[2]).wait()

        pltpu.make_async_copy(landing, landing, recv_sems.at[2]).wait()

    out[...] = landing[...].reshape(channels, TILE).T


def per_device(members, windows, forward, inverse, *arrays):
    channels = members * ROWS
    per_owner = members // windows
    vmem = pl.BlockSpec(memory_space=pltpu.VMEM)
    smem = pl.BlockSpec(memory_space=pltpu.SMEM)
    return pl.pallas_call(
        functools.partial(kernel, members, windows),
        out_shape=jax.ShapeDtypeStruct((TILE, channels), jnp.float32),
        in_specs=[vmem] * 4 + [smem] + [vmem] * 2,
        out_specs=vmem,
        scratch_shapes=[
            pltpu.VMEM((members, 2 * ROWS, TILE), jnp.bfloat16),
            pltpu.VMEM((members, 2 * ROWS, TILE), jnp.bfloat16),
            pltpu.VMEM((members + ROWS, ROWS, TILE), jnp.float32),
            pltpu.VMEM((members + ROWS, 2 * ROWS, 2 * TILE), jnp.float32),
            pltpu.VMEM((members + 1, ROWS, 2 * TILE), jnp.float32),
            pltpu.VMEM((windows, per_owner * ROWS, TILE), jnp.float32),
            pltpu.VMEM((windows, per_owner * ROWS, TILE), jnp.float32),
            pltpu.VMEM((per_owner, ROWS, TILE), jnp.float32),
            pltpu.VMEM((members, ROWS, TILE), jnp.float32),
            pltpu.SemaphoreType.DMA((3,)),
            pltpu.SemaphoreType.DMA((3,)),
        ],
        compiler_params=pltpu.CompilerParams(
            collective_id=0, has_side_effects=True, vmem_limit_bytes=32 * 1024 * 1024
        ),
    )(*arrays, forward, inverse)


def solution(mesh):
    members, windows = mesh.shape["ctx"], mesh.shape["dp"]
    forward, inverse = transform_tables()

    def run(*arrays):
        return per_device(members, windows, jnp.asarray(forward), jnp.asarray(inverse), *arrays)

    return jax.shard_map(
        run,
        mesh=mesh,
        in_specs=(P("dp", "ctx", None),) * 4 + (P("dp", None),),
        out_specs=P("ctx", None),
        check_vma=False,
    )
```

time: 615 us -> 52.7 us (0.09)
  the two profiles are of different devices: /device:TPU:56 before, /device:TPU:25 now
where the time goes in v1:
time: 52.7 us; the launch traced here: 52.4 us
  Pallas kernels  45.9 us (87%)
  local copies, waits for them, and re-layouts  6.48 us (12%)
    pallas_call x1, Pallas kernels, per_device(): pl.pallas_call(functools.partial(kernel, members, windows), out_shape=jax...  45.9 us
    unnamed x15, local copies, waits for them, and re-layouts  6.48 us

profile of v1, /device:TPU:25, one launch (start us, length us, event | category | flops | bytes accessed | tf_op | source)
XLA Modules:
  0.0 52.4 jit_solution(13733316226923788799)
XLA Ops:
  0.0 0.0 copy-start
  0.0 0.9 %copy-done = bf16[2,256,128]{2,1,0:T(8,128)(2,1)S(1)} copy-done((bf16[2,256,128]{2,1,0:T(8,128)(2,1)S(1)}, bf16[2,256,128]{2,1,0:T(8,128)(2,1)}, u32[]{:S(2)}) %copy-start) | copy-done | bytes 131096
  0.9 0.0 copy-start.1
  0.9 0.9 %copy-done.1 = bf16[2,128,256]{2,1,0:T(8,128)(2,1)S(1)} copy-done((bf16[2,128,256]{2,1,0:T(8,128)(2,1)S(1)}, bf16[2,128,256]{2,1,0:T(8,128)(2,1)}, u32[]{:S(2)}) %copy-start.1) | copy-done | bytes 131096
  1.8 0.0 copy-start.2
  1.8 0.8 %copy-done.2 = bf16[1,128,256]{2,1,0:T(8,128)(2,1)S(1)} copy-done((bf16[1,128,256]{2,1,0:T(8,128)(2,1)S(1)}, bf16[1,128,256]{2,1,0:T(8,128)(2,1)}, u32[]{:S(2)}) %copy-start.2) | copy-done | bytes 65560
  2.6 0.0 copy-start.3
  2.7 0.8 %copy-done.3 = bf16[1,128,256]{2,1,0:T(8,128)(2,1)S(1)} copy-done((bf16[1,128,256]{2,1,0:T(8,128)(2,1)S(1)}, bf16[1,128,256]{2,1,0:T(8,128)(2,1)}, u32[]{:S(2)}) %copy-start.3) | copy-done | bytes 65560
  3.5 0.0 copy-start.4
  3.5 0.8 %copy-done.4 = bf16[1,128,256]{2,1,0:T(8,128)(2,1)S(1)} copy-done((bf16[1,128,256]{2,1,0:T(8,128)(2,1)S(1)}, bf16[1,128,256]{2,1,0:T(8,128)(2,1)}, u32[]{:S(2)}) %copy-start.4) | copy-done | bytes 65560
  4.3 0.0 copy-start.5
  4.3 0.8 %copy-done.5 = bf16[1,128,256]{2,1,0:T(8,128)(2,1)S(1)} copy-done((bf16[1,128,256]{2,1,0:T(8,128)(2,1)S(1)}, bf16[1,128,256]{2,1,0:T(8,128)(2,1)}, u32[]{:S(2)}) %copy-start.5) | copy-done | bytes 65560
  5.2 0.0 copy-start.6
  5.2 0.7 %copy-done.6 = s32[1,4]{1,0:T(1,128)S(1)} copy-done((s32[1,4]{1,0:T(1,128)S(1)}, s32[1,4]{1,0:T(1,128)}, u32[]{:S(2)}) %copy-start.6) | copy-done | bytes 40
  5.8 45.9 %shard_map.73 = f32[128,256]{1,0:T(8,128)S(1)} custom-call(bf16[1,128,256]{2,1,0:T(8,128)(2,1)S(1)} %copy-done.2, bf16[1,128,256]{2,1,0:T(8,128)(2,1)S(1)} %copy-done.3, bf16[1,128,256]{2,1,0:T(8,128)(2,1)S(1)} %copy-done.4, bf16[1,128,256]{2,1,0:T(8,128)(2,1)S(1)} %copy-done.5, s32[1,4]{1,0:T(1,128)S(1)} %copy-done.6, bf16[2,128,256]{2,1,0:T(8,128)(2,1)S(1)} %copy-done.1, ...), custom_call_target="tpu_custom_call" | custom-call | tf_op jit(solution)/shard_map/pallas_call | solution.py:201
  51.7 0.7 %copy.9 = f32[128,256]{1,0:T(8,128)} copy(f32[128,256]{1,0:T(8,128)S(1)} %shard_map.73) | data formatting | bytes 262144
Async XLA Ops:
  0.0 0.9 %copy-start = (bf16[2,256,128]{2,1,0:T(8,128)(2,1)S(1)}, bf16[2,256,128]{2,1,0:T(8,128)(2,1)}, u32[]{:S(2)}) copy-start(bf16[2,256,128]{2,1,0:T(8,128)(2,1)} %constant.5.clone.inverse) | copy-start | bytes 393220
  0.9 0.9 %copy-start.1 = (bf16[2,128,256]{2,1,0:T(8,128)(2,1)S(1)}, bf16[2,128,256]{2,1,0:T(8,128)(2,1)}, u32[]{:S(2)}) copy-start(bf16[2,128,256]{2,1,0:T(8,128)(2,1)} %constant.4.clone.forward) | copy-start | bytes 393220
  1.8 0.8 %copy-start.2 = (bf16[1,128,256]{2,1,0:T(8,128)(2,1)S(1)}, bf16[1,128,256]{2,1,0:T(8,128)(2,1)}, u32[]{:S(2)}) copy-start(bf16[1,128,256]{2,1,0:T(8,128)(2,1)} %out_grad.1) | copy-start | bytes 196612
  2.6 0.8 %copy-start.3 = (bf16[1,128,256]{2,1,0:T(8,128)(2,1)S(1)}, bf16[1,128,256]{2,1,0:T(8,128)(2,1)}, u32[]{:S(2)}) copy-start(bf16[1,128,256]{2,1,0:T(8,128)(2,1)} %gate_out.1) | copy-start | bytes 196612
  3.5 0.8 %copy-start.4 = (bf16[1,128,256]{2,1,0:T(8,128)(2,1)S(1)}, bf16[1,128,256]{2,1,0:T(8,128)(2,1)}, u32[]{:S(2)}) copy-start(bf16[1,128,256]{2,1,0:T(8,128)(2,1)} %gate_in.1) | copy-start | bytes 196612
  4.3 0.8 %copy-start.5 = (bf16[1,128,256]{2,1,0:T(8,128)(2,1)S(1)}, bf16[1,128,256]{2,1,0:T(8,128)(2,1)}, u32[]{:S(2)}) copy-start(bf16[1,128,256]{2,1,0:T(8,128)(2,1)} %values.1) | copy-start | bytes 196612
  5.2 0.7 %copy-start.6 = (s32[1,4]{1,0:T(1,128)S(1)}, s32[1,4]{1,0:T(1,128)}, u32[]{:S(2)}) copy-start(s32[1,4]{1,0:T(1,128)} %doc_tiles.1) | copy-start | bytes 52

commit v2 on v1

v2 whole, which is shorter than its diff:
```python
import functools

import jax
import jax.numpy as jnp
import numpy as np
from jax import lax
from jax.experimental import pallas as pl
from jax.experimental.pallas import tpu as pltpu
from jax.sharding import PartitionSpec as P

TILE = 128
ROWS = 8
MESH = pl.DeviceIdType.MESH


def transform_tables():
    positions = np.arange(TILE)
    theta = 2.0 * np.pi * (np.arange(TILE) + 0.5) / (2 * TILE)
    forward = np.concatenate(
        [np.cos(positions[:, None] * theta), -np.sin(positions[:, None] * theta)], axis=1
    )
    inverse = np.concatenate(
        [np.cos(theta[:, None] * positions), -np.sin(theta[:, None] * positions)], axis=0
    )
    inverse = inverse / TILE
    split = []
    for table in (forward, inverse):
        table = table.astype(np.float32)
        high = table.astype(jnp.bfloat16)
        split += [high, (table - high.astype(np.float32)).astype(jnp.bfloat16)]
    return split


def product(left, right):
    return jnp.dot(left, right, preferred_element_type=jnp.float32)


def wrap(index, size):
    return lax.rem(index + 8 * size, size)


def owner_of(lag, member, ring):
    slot, row, low = lag // (2 * ring), lag // 2 % ring, lag % 2
    gap = row - member // 2 % ring
    core = member % 2
    if slot == 0:
        depth = jnp.where(core == 0, gap, 5 - gap)
    else:
        depth = jnp.where(core == 0, 1 - gap, gap - 4)
    return low * ring + wrap(depth, ring)


def lag_of(window, member, slot, ring):
    low, depth = window // ring, window % ring
    core = member % 2
    if slot == 0:
        gap = jnp.where(core == 0, depth, 5 - depth)
    else:
        gap = jnp.where(core == 0, 1 - depth, depth + 4)
    row = wrap(member // 2 % ring + gap, ring)
    return (slot * ring + row) * 2 + low


def remote(source, target, send_sem, recv_sem, **place):
    return pltpu.make_async_remote_copy(
        src_ref=source, dst_ref=target, send_sem=send_sem, recv_sem=recv_sem,
        device_id=place, device_id_type=MESH,
    )


def wait_bytes(ref, sem):
    pltpu.make_async_copy(ref, ref, sem).wait()


def kernel(
    members, windows, out_grad, gate_out, gate_in, values, doc_tiles, fwd_high, fwd_low, inv_high, inv_low, out,
    og, go, gi, va, lengths, fwd, inv,
    outgoing, incoming, docs, spectra, sums, lags, parts, total, landing,
    load_sems, tile_send, tile_recv, lag_send, lag_recv, last_send, last_recv,
):
    me = lax.axis_index("ctx")
    window = lax.axis_index("dp")
    ring = windows // 2
    channels = members * ROWS
    my_half, my_row, my_core = me // (2 * ring), me // 2 % ring, me % 2

    def member_at(half, row, core):
        return (lax.rem(my_half + half, 2) * ring + lax.rem(my_row + row, ring)) * 2 + lax.rem(
            my_core + core, 2
        )

    gaps = [[0] + ([1, ring - 1] if ring > 2 else [1])]
    gaps += [[gap, ring - gap] for gap in range(2, ring // 2)]
    gaps += [[ring // 2]] if ring > 2 else []
    groups = [
        [(half, gap, core) for gap in group for half in (1, 0) for core in (0, 1) if half + gap + core]
        for group in gaps
    ]
    far_first = [place for group in reversed(groups) for place in reversed(group)]

    barrier = pltpu.get_barrier_semaphore()
    for place in far_first:
        pl.semaphore_signal(barrier, 1, device_id={"ctx": member_at(*place)}, device_id_type=MESH)
    for step in range(1, windows):
        pl.semaphore_signal(
            barrier, 1, device_id={"dp": lax.rem(window + step, windows)}, device_id_type=MESH
        )
    pairs = [
        (out_grad, og), (gate_out, go), (gate_in, gi), (values, va), (doc_tiles, lengths),
        (fwd_high, fwd.at[pl.ds(0, TILE)]), (fwd_low, fwd.at[pl.ds(TILE, TILE)]),
        (inv_high, inv.at[0]), (inv_low, inv.at[1]),
    ]
    loads = [
        pltpu.make_async_copy(source, target, load_sems.at[n]) for n, (source, target) in enumerate(pairs)
    ]
    for load in loads:
        load.start()
    for load in loads:
        load.wait()

    weighted = go[0].astype(jnp.float32) * og[0].astype(jnp.float32)
    gated = gi[0].astype(jnp.float32) * va[0].astype(jnp.float32)
    weighted = weighted.T.reshape(members, 1, ROWS, TILE)
    gated = gated.T.reshape(members, 1, ROWS, TILE)
    outgoing[...] = (
        jnp.concatenate([weighted, gated], axis=1)
        .reshape(members, 2 * ROWS, TILE)
        .astype(jnp.bfloat16)
    )
    incoming[me] = outgoing[me]

    tile = lax.broadcasted_iota(jnp.int32, docs.shape, 0)
    label = jnp.zeros(docs.shape, jnp.float32)
    end = jnp.int32(0)
    for entry in range(lengths.shape[1]):
        end = end + lengths[0, entry]
        label += (tile >= end).astype(jnp.float32)
    docs[...] = label
    spectra[pl.ds(members, ROWS)] = jnp.zeros((ROWS, 2 * ROWS, 2 * TILE), jnp.float32)
    sums[members] = jnp.zeros((ROWS, 2 * TILE), jnp.float32)

    pl.semaphore_wait(barrier, members + windows - 2)

    for number in reversed(range(len(groups))):
        for place in reversed(groups[number]):
            peer = member_at(*place)
            remote(
                outgoing.at[peer], incoming.at[me], tile_send, tile_recv.at[number], ctx=peer
            ).start()
    for number, group in enumerate(groups):
        wait_bytes(incoming.at[pl.ds(0, len(group))], tile_recv.at[number])
        places = sorted({(half, gap) for half, gap, _ in group})
        if number == 0:
            places = sorted(set(places) | {(0, 0)})
        starts = [
            (lax.rem(my_half + half, 2) * ring + lax.rem(my_row + gap, ring)) * 2 for half, gap in places
        ]
        tiles = jnp.concatenate(
            [incoming[pl.ds(start, 2)].reshape(4 * ROWS, TILE) for start in starts], axis=0
        )
        hats = product(jnp.concatenate([tiles, tiles], axis=1), fwd[...])
        for number_, start in enumerate(starts):
            spectra[pl.ds(start, 2)] = hats[number_ * 4 * ROWS : (number_ + 1) * 4 * ROWS].reshape(
                2, 2 * ROWS, 2 * TILE
            )

    def add_pairs(first, stop, terms):
        def lag_block(lag, carried):
            real = jnp.zeros((ROWS, TILE), jnp.float32)
            imag = jnp.zeros((ROWS, TILE), jnp.float32)
            for source in range(terms):
                head = source + lag
                head_real = spectra[head, :ROWS, :TILE]
                head_imag = spectra[head, :ROWS, TILE:]
                tail_real = spectra[source, ROWS:, :TILE]
                tail_imag = spectra[source, ROWS:, TILE:]
                same = docs[head] == docs[source]
                real += jnp.where(same, head_real * tail_real + head_imag * tail_imag, 0.0)
                imag += jnp.where(same, head_imag * tail_real - head_real * tail_imag, 0.0)
            sums[lag, :, :TILE] = real
            sums[lag, :, TILE:] = imag
            return carried

        lax.fori_loop(first, stop, lag_block, 0)

    parity = lax.broadcasted_iota(jnp.int32, (members // 2 * ROWS, TILE), 1) % 2
    sign = (1 - 2 * parity).astype(jnp.float32)

    def back_and_send(slot):
        half = members // 2
        here = sums[pl.ds(slot * half, half)].reshape(half * ROWS, 2 * TILE)
        after = sums[pl.ds(slot * half + 1, half)].reshape(half * ROWS, 2 * TILE)
        both = jnp.concatenate(
            [here[:, :TILE] + sign * after[:, TILE:], here[:, TILE:] - sign * after[:, :TILE]], axis=1
        )
        high = both.astype(jnp.bfloat16)
        low = (both - high.astype(jnp.float32)).astype(jnp.bfloat16)
        result = product(high, inv[0]) + product(low, inv[0]) + product(high, inv[1])
        lags[pl.ds(slot * half, half)] = result.reshape(half, ROWS, TILE)
        for lag in range(slot * half, (slot + 1) * half):
            owner = owner_of(lag, me, ring)

            @pl.when(owner != window)
            def _():
                remote(
                    lags.at[lag], parts.at[slot, window], lag_send, lag_recv.at[slot], dp=owner
                ).start()

        parts[slot, window] = lags[lag_of(window, me, slot, ring)]

    half = members // 2
    quarter = members // 4
    add_pairs(0, quarter, members)
    add_pairs(quarter, half + 1, members - quarter)
    back_and_send(0)
    add_pairs(half + 1, half + quarter, half)
    add_pairs(half + quarter, members, quarter)
    back_and_send(1)

    others = pl.ds(0, windows - 1)
    for slot in range(2):
        wait_bytes(parts.at[slot, others], lag_recv.at[slot])
        total[slot] = jnp.sum(parts[slot], axis=0)
        lag = lag_of(window, me, slot, ring)
        for depth in range(ring):
            for low in range(2):
                reader = low * ring + depth
                own = (reader == window) & (lag == me)

                @pl.when(own)
                def _():
                    pltpu.make_async_copy(total.at[slot], landing.at[me], last_recv).start()

                @pl.when(jnp.logical_not(own))
                def _():
                    remote(
                        total.at[slot], landing.at[me], last_send, last_recv, ctx=lag, dp=reader
                    ).start()

    wait_bytes(landing, last_recv)
    out[...] = landing[...].reshape(channels, TILE).T

    wait_bytes(outgoing.at[pl.ds(0, members - 1)], tile_send)
    wait_bytes(lags.at[pl.ds(0, members - 2)], lag_send)
    keeps = (lag_of(window, me, 0, ring) == me) | (lag_of(window, me, 1, ring) == me)

    @pl.when(keeps)
    def _():
        wait_bytes(landing.at[pl.ds(0, members - 1)], last_send)

    @pl.when(jnp.logical_not(keeps))
    def _():
        wait_bytes(landing, last_send)


def per_device(members, windows, tables, *arrays):
    channels = members * ROWS
    hbm = pl.BlockSpec(memory_space=pltpu.HBM)
    return pl.pallas_call(
        functools.partial(kernel, members, windows),
        out_shape=pltpu.VMEM((TILE, channels), jnp.float32),
        in_specs=[hbm] * 9,
        out_specs=pl.BlockSpec(memory_space=pltpu.VMEM),
        scratch_shapes=[
            pltpu.VMEM((1, TILE, channels), jnp.bfloat16),
            pltpu.VMEM((1, TILE, channels), jnp.bfloat16),
            pltpu.VMEM((1, TILE, channels), jnp.bfloat16),
            pltpu.VMEM((1, TILE, channels), jnp.bfloat16),
            pltpu.SMEM(arrays[4].shape, jnp.int32),
            pltpu.VMEM((2 * TILE, 2 * TILE), jnp.bfloat16),
            pltpu.VMEM((2, 2 * TILE, TILE), jnp.bfloat16),
            pltpu.VMEM((members, 2 * ROWS, TILE), jnp.bfloat16),
            pltpu.VMEM((members, 2 * ROWS, TILE), jnp.bfloat16),
            pltpu.VMEM((members + ROWS, ROWS, TILE), jnp.float32),
            pltpu.VMEM((members + ROWS, 2 * ROWS, 2 * TILE), jnp.float32),
            pltpu.VMEM((members + 1, ROWS, 2 * TILE), jnp.float32),
            pltpu.VMEM((members, ROWS, TILE), jnp.float32),
            pltpu.VMEM((2, windows, ROWS, TILE), jnp.float32),
            pltpu.VMEM((2, ROWS, TILE), jnp.float32),
            pltpu.VMEM((members, ROWS, TILE), jnp.float32),
            pltpu.SemaphoreType.DMA((9,)),
            pltpu.SemaphoreType.DMA,
            pltpu.SemaphoreType.DMA((4,)),
            pltpu.SemaphoreType.DMA,
            pltpu.SemaphoreType.DMA((2,)),
            pltpu.SemaphoreType.DMA,
            pltpu.SemaphoreType.DMA,
        ],
        compiler_params=pltpu.CompilerParams(
            collective_id=0, has_side_effects=True, vmem_limit_bytes=60 * 1024 * 1024
        ),
    )(*[pltpu.with_memory_space_constraint(array, pltpu.HBM) for array in (*arrays, *tables)])


def solution(mesh):
    members, windows = mesh.shape["ctx"], mesh.shape["dp"]
    tables = transform_tables()

    def run(*arrays):
        return per_device(members, windows, [jnp.asarray(table) for table in tables], *arrays)

    return jax.shard_map(
        run,
        mesh=mesh,
        in_specs=(P("dp", "ctx", None),) * 4 + (P("dp", None),),
        out_specs=P("ctx", None),
        check_vma=False,
    )
```

time: 52.7 us -> 38.8 us (0.74)
  the two profiles are of different devices: /device:TPU:25 before, /device:TPU:1 now
where the time goes in v2:
time: 38.8 us; the launch traced here: 38.1 us
  Pallas kernels  37.5 us (97%)
  local copies, waits for them, and re-layouts  0.66 us (2%)
    pallas_call x1, Pallas kernels, per_device(): pl.pallas_call(functools.partial(kernel, members, windows), out_shape=plt...  37.5 us

profile of v2, /device:TPU:1, one launch (start us, length us, event | category | flops | bytes accessed | tf_op | source)
XLA Modules:
  0.0 38.1 jit_solution(2593908513289866747)
XLA Ops:
  0.0 37.5 %shard_map.91 = f32[128,256]{1,0:T(8,128)S(1)} custom-call(bf16[1,128,256]{2,1,0:T(8,128)(2,1)} %out_grad.1, bf16[1,128,256]{2,1,0:T(8,128)(2,1)} %gate_out.1, bf16[1,128,256]{2,1,0:T(8,128)(2,1)} %gate_in.1, bf16[1,128,256]{2,1,0:T(8,128)(2,1)} %values.1, s32[1,4]{1,0:T(1,128)} %doc_tiles.1, bf16[128,256]{1,0:T(8,128)(2,1)} %constant.8.clone.fwd_high, ...), custom_call_target="tpu_custom_call" | custom-call | tf_op jit(solution)/shard_map/pallas_call | solution.py:259
  37.5 0.7 %copy.11 = f32[128,256]{1,0:T(8,128)} copy(f32[128,256]{1,0:T(8,128)S(1)} %shard_map.91) | data formatting | bytes 262144

commit v3 on v2

--- a/solution.py
+++ b/solution.py
@@ -39,26 +39,38 @@
     return lax.rem(index + 8 * size, size)
 
 
-def owner_of(lag, member, ring):
-    slot, row, low = lag // (2 * ring), lag // 2 % ring, lag % 2
-    gap = row - member // 2 % ring
-    core = member % 2
-    if slot == 0:
-        depth = jnp.where(core == 0, gap, 5 - gap)
-    else:
-        depth = jnp.where(core == 0, 1 - gap, gap - 4)
-    return low * ring + wrap(depth, ring)
+PLAN = [
+    [[3, 1, 0, 6, 5, 4, 2, 7], [1, 6, 5, 0, 4, 2, 3, 7], [2, 3, 6, 4, 0, 1, 5, 7], [7, 1, 3, 5, 0, 4, 6, 2]],
+    [[6, 2, 3, 0, 5, 4, 7, 1], [2, 5, 1, 0, 4, 7, 6, 3], [7, 3, 4, 6, 0, 5, 1, 2], [2, 0, 7, 4, 6, 1, 3, 5]],
+    [[3, 2, 0, 5, 6, 7, 1, 4], [5, 7, 6, 1, 3, 0, 2, 4], [4, 3, 0, 7, 1, 2, 5, 6], [1, 7, 0, 5, 6, 3, 4, 2]],
+    [[7, 5, 2, 1, 6, 3, 4, 0], [6, 7, 5, 2, 1, 3, 0, 4], [3, 4, 5, 2, 1, 7, 6, 0], [7, 5, 4, 1, 2, 6, 0, 3]],
+    [[1, 2, 7, 3, 4, 6, 5, 0], [4, 1, 2, 3, 7, 5, 6, 0], [0, 2, 6, 7, 3, 1, 4, 5], [0, 6, 2, 7, 4, 1, 3, 5]],
+    [[5, 4, 2, 7, 3, 6, 1, 0], [5, 0, 7, 4, 3, 2, 1, 6], [0, 1, 5, 4, 7, 6, 2, 3], [2, 6, 5, 7, 3, 4, 0, 1]],
+    [[1, 0, 4, 5, 7, 2, 3, 6], [4, 7, 1, 6, 5, 0, 2, 3], [6, 4, 2, 3, 7, 0, 5, 1], [3, 5, 1, 6, 4, 0, 7, 2]],
+    [[5, 6, 7, 2, 1, 3, 0, 4], [6, 0, 4, 3, 2, 5, 1, 7], [4, 3, 0, 2, 1, 6, 7, 5], [0, 4, 3, 1, 2, 7, 5, 6]],
+]
+
+
+def row_codes(ring):
+    plan = PLAN if ring == 8 else [[[(y + z) % ring for z in range(ring)] for _ in range(4)] for y in range(ring)]
+    return [
+        [[sum(plan[y][2 * slot + core][z] << 3 * y for y in range(ring)) for z in range(ring)] for core in range(2)]
+        for slot in range(2)
+    ]
+
+
+def lag_at(depth, low, member, slot, ring):
+    codes = row_codes(ring)[slot]
+    code = jnp.where(member % 2 == 0, codes[0][depth], codes[1][depth])
+    row = jnp.bitwise_and(jnp.right_shift(code, 3 * (member // 2 % ring)), 7)
+    return (slot * ring + row) * 2 + low
 
 
 def lag_of(window, member, slot, ring):
-    low, depth = window // ring, window % ring
-    core = member % 2
-    if slot == 0:
-        gap = jnp.where(core == 0, depth, 5 - depth)
-    else:
-        gap = jnp.where(core == 0, 1 - depth, depth + 4)
-    row = wrap(member // 2 % ring + gap, ring)
-    return (slot * ring + row) * 2 + low
+    lag = lag_at(0, window // ring, member, slot, ring)
+    for depth in range(1, ring):
+        lag = jnp.where(window % ring == depth, lag_at(depth, window // ring, member, slot, ring), lag)
+    return lag
 
 
 def remote(source, target, send_sem, recv_sem, **place):
@@ -141,12 +153,19 @@
 
     pl.semaphore_wait(barrier, members + windows - 2)
 
-    for number in reversed(range(len(groups))):
-        for place in reversed(groups[number]):
-            peer = member_at(*place)
+    late_rows = sorted(range(ring), key=lambda row: min(row, ring - row), reverse=True)
+    late_first = [(row, half, core) for row in late_rows for half in range(2) for core in range(2)]
+    for row, half, core in late_first:
+        peer = (half * ring + row) * 2 + core
+        gap = wrap(row - my_row, ring)
+        number = jnp.maximum(jnp.minimum(gap, ring - gap) - 1, 0)
+
+        @pl.when(peer != me)
+        def _():
             remote(
                 outgoing.at[peer], incoming.at[me], tile_send, tile_recv.at[number], ctx=peer
             ).start()
+
     for number, group in enumerate(groups):
         wait_bytes(incoming.at[pl.ds(0, len(group))], tile_recv.at[number])
         places = sorted({(half, gap) for half, gap, _ in group})
@@ -197,14 +216,16 @@
         low = (both - high.astype(jnp.float32)).astype(jnp.bfloat16)
         result = product(high, inv[0]) + product(low, inv[0]) + product(high, inv[1])
         lags[pl.ds(slot * half, half)] = result.reshape(half, ROWS, TILE)
-        for lag in range(slot * half, (slot + 1) * half):
-            owner = owner_of(lag, me, ring)
-
-            @pl.when(owner != window)
-            def _():
-                remote(
-                    lags.at[lag], parts.at[slot, window], lag_send, lag_recv.at[slot], dp=owner
-                ).start()
+        for depth in late_rows:
+            for low in range(2):
+                owner = low * ring + depth
+
+                @pl.when(owner != window)
+                def _():
+                    remote(
+                        lags.at[lag_at(depth, low, me, slot, ring)], parts.at[slot, window],
+                        lag_send, lag_recv.at[slot], dp=owner,
+                    ).start()
 
         parts[slot, window] = lags[lag_of(window, me, slot, ring)]
 

time: 38.8 us -> 37.5 us (0.966); the launches traced: 38.1 us -> 37.3 us
  Pallas kernels: 37.5 us -> 36.6 us
    pallas_call x1, Pallas kernels: 37.5 us -> 36.6 us  [per_device(): pl.pallas_call(functools.partial(kernel, members, windows), out_shape=plt...]
where the time goes in v3:
time: 37.5 us; the launch traced here: 37.3 us
  Pallas kernels  36.6 us (98%)
  local copies, waits for them, and re-layouts  0.66 us (2%)
    pallas_call x1, Pallas kernels, per_device(): pl.pallas_call(functools.partial(kernel, members, windows), out_shape=plt...  36.6 us

profile of v3, /device:TPU:1, one launch (start us, length us, event | category | flops | bytes accessed | tf_op | source)
XLA Modules:
  0.0 37.3 jit_solution(5531752145706424414)
XLA Ops:
  0.0 36.6 %shard_map.91 = f32[128,256]{1,0:T(8,128)S(1)} custom-call(bf16[1,128,256]{2,1,0:T(8,128)(2,1)} %out_grad.1, bf16[1,128,256]{2,1,0:T(8,128)(2,1)} %gate_out.1, bf16[1,128,256]{2,1,0:T(8,128)(2,1)} %gate_in.1, bf16[1,128,256]{2,1,0:T(8,128)(2,1)} %values.1, s32[1,4]{1,0:T(1,128)} %doc_tiles.1, bf16[128,256]{1,0:T(8,128)(2,1)} %constant.8.clone.fwd_high, ...), custom_call_target="tpu_custom_call" | custom-call | tf_op jit(solution)/shard_map/pallas_call | solution.py:280
  36.6 0.7 %copy.11 = f32[128,256]{1,0:T(8,128)} copy(f32[128,256]{1,0:T(8,128)S(1)} %shard_map.91) | data formatting | bytes 262144

commit v4 on v2

--- a/solution.py
+++ b/solution.py
@@ -39,26 +39,60 @@
     return lax.rem(index + 8 * size, size)
 
 
-def owner_of(lag, member, ring):
-    slot, row, low = lag // (2 * ring), lag // 2 % ring, lag % 2
-    gap = row - member // 2 % ring
-    core = member % 2
-    if slot == 0:
-        depth = jnp.where(core == 0, gap, 5 - gap)
-    else:
-        depth = jnp.where(core == 0, 1 - gap, gap - 4)
-    return low * ring + wrap(depth, ring)
+PLAN = [
+    [
+        [[7, 6, 2, 4, 5, 1, 0, 3], [5, 2, 4, 3, 1, 6, 7, 0], [3, 0, 4, 5, 6, 2, 1, 7], [1, 2, 5, 6, 0, 7, 3, 4]],
+        [[1, 7, 5, 0, 4, 3, 6, 2], [2, 1, 0, 5, 4, 6, 3, 7], [3, 5, 7, 1, 0, 4, 6, 2], [7, 5, 4, 3, 0, 2, 1, 6]],
+        [[4, 2, 3, 0, 6, 7, 5, 1], [7, 5, 2, 6, 3, 4, 1, 0], [2, 4, 0, 1, 6, 5, 7, 3], [4, 7, 2, 6, 1, 0, 3, 5]],
+        [[3, 6, 7, 5, 1, 0, 4, 2], [5, 2, 3, 1, 7, 6, 0, 4], [5, 0, 4, 2, 3, 1, 6, 7], [0, 3, 1, 4, 7, 2, 5, 6]],
+        [[4, 3, 1, 2, 5, 7, 6, 0], [0, 1, 6, 7, 2, 5, 3, 4], [0, 1, 6, 7, 5, 3, 4, 2], [6, 7, 5, 4, 3, 2, 1, 0]],
+        [[1, 5, 3, 2, 7, 4, 0, 6], [0, 4, 1, 5, 2, 7, 6, 3], [1, 0, 2, 7, 6, 3, 4, 5], [5, 0, 7, 3, 4, 6, 2, 1]],
+        [[2, 6, 5, 3, 7, 1, 0, 4], [6, 1, 0, 4, 7, 3, 2, 5], [2, 4, 1, 6, 3, 5, 0, 7], [3, 2, 6, 7, 5, 1, 4, 0]],
+        [[6, 3, 7, 2, 4, 0, 5, 1], [6, 7, 3, 0, 1, 4, 2, 5], [7, 4, 6, 1, 2, 0, 5, 3], [4, 7, 0, 1, 2, 5, 3, 6]],
+    ],
+    [
+        [[5, 6, 4, 0, 3, 1, 7, 2], [2, 6, 0, 3, 4, 5, 1, 7], [7, 5, 3, 1, 4, 0, 2, 6], [0, 1, 7, 3, 2, 4, 6, 5]],
+        [[4, 2, 6, 1, 5, 7, 0, 3], [7, 2, 6, 5, 0, 4, 3, 1], [3, 7, 0, 6, 1, 2, 5, 4], [6, 3, 2, 5, 4, 1, 0, 7]],
+        [[3, 5, 1, 7, 6, 0, 4, 2], [2, 4, 5, 1, 7, 3, 6, 0], [5, 3, 4, 7, 1, 0, 6, 2], [2, 0, 1, 5, 7, 6, 3, 4]],
+        [[0, 4, 7, 6, 2, 1, 3, 5], [6, 0, 1, 2, 3, 5, 7, 4], [5, 0, 1, 2, 4, 7, 6, 3], [3, 6, 4, 5, 2, 7, 1, 0]],
+        [[1, 6, 2, 3, 5, 7, 4, 0], [0, 4, 7, 3, 5, 2, 1, 6], [1, 7, 2, 4, 3, 6, 5, 0], [0, 1, 7, 3, 6, 2, 4, 5]],
+        [[0, 1, 6, 7, 3, 5, 4, 2], [6, 0, 5, 3, 7, 4, 2, 1], [4, 2, 5, 7, 3, 6, 0, 1], [5, 4, 3, 6, 7, 2, 1, 0]],
+        [[2, 5, 1, 4, 7, 0, 3, 6], [2, 3, 0, 4, 7, 1, 6, 5], [1, 0, 3, 7, 6, 5, 2, 4], [6, 2, 4, 7, 5, 3, 0, 1]],
+        [[4, 1, 5, 2, 0, 6, 7, 3], [4, 6, 2, 0, 1, 3, 5, 7], [7, 1, 0, 6, 4, 2, 5, 3], [1, 7, 3, 4, 5, 0, 2, 6]],
+    ],
+]
+
+
+def plan_row(half, slot, core, depth, y, ring):
+    return PLAN[half][y][2 * slot + core][depth] if ring == 8 else (y + depth) % ring
+
+
+def select(codes, member, ring):
+    code = jnp.where(member % 2 == 0, codes[0], codes[1])
+    return jnp.bitwise_and(jnp.right_shift(code, 3 * (member // 2 % ring)), 7)
+
+
+def depth_at(half, row, member, slot, ring):
+    codes = []
+    for core in range(2):
+        rows = [[plan_row(half, slot, core, depth, y, ring) for depth in range(ring)] for y in range(ring)]
+        codes.append(sum(rows[y].index(row) << 3 * y for y in range(ring)))
+    return select(codes, member, ring)
+
+
+def lag_at(half, depth, member, slot, ring):
+    codes = [
+        sum(plan_row(half, slot, core, depth, y, ring) << 3 * y for y in range(ring)) for core in range(2)
+    ]
+    return (half * ring + select(codes, member, ring)) * 2 + slot
 
 
 def lag_of(window, member, slot, ring):
-    low, depth = window // ring, window % ring
-    core = member % 2
-    if slot == 0:
-        gap = jnp.where(core == 0, depth, 5 - depth)
-    else:
-        gap = jnp.where(core == 0, 1 - depth, depth + 4)
-    row = wrap(member // 2 % ring + gap, ring)
-    return (slot * ring + row) * 2 + low
+    mine = lax.rem(window // ring + member // (2 * ring), 2) * ring + window % ring
+    lag = lag_at(0, 0, member, slot, ring)
+    for place in range(1, 2 * ring):
+        lag = jnp.where(mine == place, lag_at(place // ring, place % ring, member, slot, ring), lag)
+    return lag
 
 
 def remote(source, target, send_sem, recv_sem, **place):
@@ -76,7 +110,7 @@
     members, windows, out_grad, gate_out, gate_in, values, doc_tiles, fwd_high, fwd_low, inv_high, inv_low, out,
     og, go, gi, va, lengths, fwd, inv,
     outgoing, incoming, docs, spectra, sums, lags, parts, total, landing,
-    load_sems, tile_send, tile_recv, lag_send, lag_recv, last_send, last_recv,
+    load_sems, tile_send, tile_recv, lag_send, lag_recv, last_send, last_recv, window_sem,
 ):
     me = lax.axis_index("ctx")
     window = lax.axis_index("dp")
@@ -101,10 +135,15 @@
     barrier = pltpu.get_barrier_semaphore()
     for place in far_first:
         pl.semaphore_signal(barrier, 1, device_id={"ctx": member_at(*place)}, device_id_type=MESH)
-    for step in range(1, windows):
-        pl.semaphore_signal(
-            barrier, 1, device_id={"dp": lax.rem(window + step, windows)}, device_id_type=MESH
-        )
+    early = window % ring < ring // 2
+    for depth in reversed(range(ring)):
+        for low in range(2):
+            known = depth >= ring // 2
+
+            @pl.when((low * ring + depth != window) & (early | known))
+            def _():
+                pl.semaphore_signal(barrier, 1, device_id={"dp": low * ring + depth}, device_id_type=MESH)
+
     pairs = [
         (out_grad, og), (gate_out, go), (gate_in, gi), (values, va), (doc_tiles, lengths),
         (fwd_high, fwd.at[pl.ds(0, TILE)]), (fwd_low, fwd.at[pl.ds(TILE, TILE)]),
@@ -139,14 +178,27 @@
     spectra[pl.ds(members, ROWS)] = jnp.zeros((ROWS, 2 * ROWS, 2 * TILE), jnp.float32)
     sums[members] = jnp.zeros((ROWS, 2 * TILE), jnp.float32)
 
-    pl.semaphore_wait(barrier, members + windows - 2)
-
-    for number in reversed(range(len(groups))):
-        for place in reversed(groups[number]):
-            peer = member_at(*place)
+    pl.semaphore_wait(barrier, members - 1 + jnp.where(early, ring - 1, windows - 1))
+
+    late_rows = sorted(range(ring), key=lambda row: min(row, ring - row), reverse=True)
+    late_first = [(row, half, core) for row in late_rows for half in range(2) for core in range(2)]
+    for row, half, core in late_first:
+        peer = (half * ring + row) * 2 + core
+        gap = wrap(row - my_row, ring)
+        number = jnp.maximum(jnp.minimum(gap, ring - gap) - 1, 0)
+
+        @pl.when(peer != me)
+        def _():
             remote(
                 outgoing.at[peer], incoming.at[me], tile_send, tile_recv.at[number], ctx=peer
             ).start()
+
+    @pl.when(jnp.logical_not(early))
+    def _():
+        for depth in range(ring // 2):
+            for low in range(2):
+                pl.semaphore_signal(window_sem, 1, device_id={"dp": low * ring + depth}, device_id_type=MESH)
+
     for number, group in enumerate(groups):
         wait_bytes(incoming.at[pl.ds(0, len(group))], tile_recv.at[number])
         places = sorted({(half, gap) for half, gap, _ in group})
@@ -183,22 +235,25 @@
 
         lax.fori_loop(first, stop, lag_block, 0)
 
-    parity = lax.broadcasted_iota(jnp.int32, (members // 2 * ROWS, TILE), 1) % 2
+    quarter = members // 4
+    parity = lax.broadcasted_iota(jnp.int32, (quarter * ROWS, TILE), 1) % 2
     sign = (1 - 2 * parity).astype(jnp.float32)
 
-    def back_and_send(slot):
-        half = members // 2
-        here = sums[pl.ds(slot * half, half)].reshape(half * ROWS, 2 * TILE)
-        after = sums[pl.ds(slot * half + 1, half)].reshape(half * ROWS, 2 * TILE)
+    def back_and_send(first):
+        here = sums[pl.ds(first, quarter)].reshape(quarter * ROWS, 2 * TILE)
+        after = sums[pl.ds(first + 1, quarter)].reshape(quarter * ROWS, 2 * TILE)
         both = jnp.concatenate(
             [here[:, :TILE] + sign * after[:, TILE:], here[:, TILE:] - sign * after[:, :TILE]], axis=1
         )
         high = both.astype(jnp.bfloat16)
         low = (both - high.astype(jnp.float32)).astype(jnp.bfloat16)
         result = product(high, inv[0]) + product(low, inv[0]) + product(high, inv[1])
-        lags[pl.ds(slot * half, half)] = result.reshape(half, ROWS, TILE)
-        for lag in range(slot * half, (slot + 1) * half):
-            owner = owner_of(lag, me, ring)
+        lags[pl.ds(first, quarter)] = result.reshape(quarter, ROWS, TILE)
+        half = first // (2 * ring)
+        base = lax.rem(half + my_half, 2) * ring
+        for lag in range(first, first + quarter):
+            slot = lag % 2
+            owner = base + depth_at(half, lag // 2 % ring, me, slot, ring)
 
             @pl.when(owner != window)
             def _():
@@ -206,23 +261,28 @@
                     lags.at[lag], parts.at[slot, window], lag_send, lag_recv.at[slot], dp=owner
                 ).start()
 
-        parts[slot, window] = lags[lag_of(window, me, slot, ring)]
-
-    half = members // 2
-    quarter = members // 4
-    add_pairs(0, quarter, members)
-    add_pairs(quarter, half + 1, members - quarter)
+    add_pairs(0, quarter + 1, members)
+
+    @pl.when(early)
+    def _():
+        pl.semaphore_wait(window_sem, ring)
+
     back_and_send(0)
-    add_pairs(half + 1, half + quarter, half)
-    add_pairs(half + quarter, members, quarter)
-    back_and_send(1)
-
-    others = pl.ds(0, windows - 1)
+    add_pairs(quarter + 1, 2 * quarter + 1, members - quarter)
+    back_and_send(quarter)
+    add_pairs(2 * quarter + 1, 3 * quarter + 1, 2 * quarter)
+    back_and_send(2 * quarter)
+    add_pairs(3 * quarter + 1, members, quarter)
+    back_and_send(3 * quarter)
+
+    mine = [lag_of(window, me, slot, ring) for slot in range(2)]
     for slot in range(2):
-        wait_bytes(parts.at[slot, others], lag_recv.at[slot])
-        total[slot] = jnp.sum(parts[slot], axis=0)
-        lag = lag_of(window, me, slot, ring)
-        for depth in range(ring):
+        parts[slot, window] = lags[mine[slot]]
+    lead = (mine[1] // 2 <= mine[0] // 2).astype(jnp.int32)
+
+    def spread(slot, depths):
+        lag = jnp.where(slot == 0, mine[0], mine[1])
+        for depth in depths:
             for low in range(2):
                 reader = low * ring + depth
                 own = (reader == window) & (lag == me)
@@ -237,12 +297,20 @@
                         total.at[slot], landing.at[me], last_send, last_recv, ctx=lag, dp=reader
                     ).start()
 
+    for slot in (lead, 1 - lead):
+        wait_bytes(parts.at[slot, pl.ds(0, windows - 1)], lag_recv.at[slot])
+        total[slot] = jnp.sum(parts[slot], axis=0)
+        spread(slot, range(2))
+    for depth in range(2, ring):
+        spread(lead, [depth])
+        spread(1 - lead, [depth])
+
     wait_bytes(landing, last_recv)
     out[...] = landing[...].reshape(channels, TILE).T
 
     wait_bytes(outgoing.at[pl.ds(0, members - 1)], tile_send)
     wait_bytes(lags.at[pl.ds(0, members - 2)], lag_send)
-    keeps = (lag_of(window, me, 0, ring) == me) | (lag_of(window, me, 1, ring) == me)
+    keeps = (mine[0] == me) | (mine[1] == me)
 
     @pl.when(keeps)
     def _():
@@ -285,6 +353,7 @@
             pltpu.SemaphoreType.DMA((2,)),
             pltpu.SemaphoreType.DMA,
             pltpu.SemaphoreType.DMA,
+            pltpu.SemaphoreType.REGULAR,
         ],
         compiler_params=pltpu.CompilerParams(
             collective_id=0, has_side_effects=True, vmem_limit_bytes=60 * 1024 * 1024

time: 38.8 us -> 36.4 us (0.938); the launches traced: 38.1 us -> 36.3 us
  Pallas kernels: 37.5 us -> 35.6 us
    pallas_call x1, Pallas kernels: 37.5 us -> 35.6 us  [per_device(): pl.pallas_call(functools.partial(kernel, members, windows), out_shape=plt...]
where the time goes in v4:
time: 36.4 us; the launch traced here: 36.3 us
  Pallas kernels  35.6 us (98%)
  local copies, waits for them, and re-layouts  0.66 us (2%)
    pallas_call x1, Pallas kernels, per_device(): pl.pallas_call(functools.partial(kernel, members, windows), out_shape=plt...  35.6 us

profile of v4, /device:TPU:1, one launch (start us, length us, event | category | flops | bytes accessed | tf_op | source)
XLA Modules:
  0.0 36.3 jit_solution(5127548388186928880)
XLA Ops:
  0.0 35.6 %shard_map.91 = f32[128,256]{1,0:T(8,128)S(1)} custom-call(bf16[1,128,256]{2,1,0:T(8,128)(2,1)} %out_grad.1, bf16[1,128,256]{2,1,0:T(8,128)(2,1)} %gate_out.1, bf16[1,128,256]{2,1,0:T(8,128)(2,1)} %gate_in.1, bf16[1,128,256]{2,1,0:T(8,128)(2,1)} %values.1, s32[1,4]{1,0:T(1,128)} %doc_tiles.1, bf16[128,256]{1,0:T(8,128)(2,1)} %constant.8.clone.fwd_high, ...), custom_call_target="tpu_custom_call" | custom-call | tf_op jit(solution)/shard_map/pallas_call | solution.py:327
  35.6 0.7 %copy.11 = f32[128,256]{1,0:T(8,128)} copy(f32[128,256]{1,0:T(8,128)S(1)} %shard_map.91) | data formatting | bytes 262144

commit v5 on v4

--- a/solution.py
+++ b/solution.py
@@ -41,24 +41,24 @@
 
 PLAN = [
     [
-        [[7, 6, 2, 4, 5, 1, 0, 3], [5, 2, 4, 3, 1, 6, 7, 0], [3, 0, 4, 5, 6, 2, 1, 7], [1, 2, 5, 6, 0, 7, 3, 4]],
-        [[1, 7, 5, 0, 4, 3, 6, 2], [2, 1, 0, 5, 4, 6, 3, 7], [3, 5, 7, 1, 0, 4, 6, 2], [7, 5, 4, 3, 0, 2, 1, 6]],
-        [[4, 2, 3, 0, 6, 7, 5, 1], [7, 5, 2, 6, 3, 4, 1, 0], [2, 4, 0, 1, 6, 5, 7, 3], [4, 7, 2, 6, 1, 0, 3, 5]],
-        [[3, 6, 7, 5, 1, 0, 4, 2], [5, 2, 3, 1, 7, 6, 0, 4], [5, 0, 4, 2, 3, 1, 6, 7], [0, 3, 1, 4, 7, 2, 5, 6]],
-        [[4, 3, 1, 2, 5, 7, 6, 0], [0, 1, 6, 7, 2, 5, 3, 4], [0, 1, 6, 7, 5, 3, 4, 2], [6, 7, 5, 4, 3, 2, 1, 0]],
-        [[1, 5, 3, 2, 7, 4, 0, 6], [0, 4, 1, 5, 2, 7, 6, 3], [1, 0, 2, 7, 6, 3, 4, 5], [5, 0, 7, 3, 4, 6, 2, 1]],
-        [[2, 6, 5, 3, 7, 1, 0, 4], [6, 1, 0, 4, 7, 3, 2, 5], [2, 4, 1, 6, 3, 5, 0, 7], [3, 2, 6, 7, 5, 1, 4, 0]],
-        [[6, 3, 7, 2, 4, 0, 5, 1], [6, 7, 3, 0, 1, 4, 2, 5], [7, 4, 6, 1, 2, 0, 5, 3], [4, 7, 0, 1, 2, 5, 3, 6]],
+        [[2, 6, 5, 0, 4, 3, 1, 7], [4, 6, 2, 0, 7, 5, 1, 3], [7, 4, 0, 3, 1, 5, 6, 2], [3, 0, 6, 1, 2, 4, 7, 5]],
+        [[6, 2, 0, 5, 1, 7, 4, 3], [7, 3, 0, 6, 5, 2, 4, 1], [0, 7, 3, 1, 5, 4, 2, 6], [2, 3, 1, 5, 4, 0, 7, 6]],
+        [[3, 2, 4, 5, 7, 0, 6, 1], [1, 0, 4, 7, 6, 2, 5, 3], [5, 4, 7, 3, 1, 6, 0, 2], [6, 0, 2, 7, 3, 5, 1, 4]],
+        [[3, 0, 4, 1, 7, 6, 2, 5], [2, 6, 7, 5, 1, 3, 0, 4], [5, 3, 1, 4, 2, 7, 0, 6], [6, 4, 7, 2, 5, 1, 3, 0]],
+        [[3, 0, 5, 6, 2, 4, 7, 1], [0, 6, 7, 4, 3, 1, 2, 5], [1, 4, 6, 2, 3, 7, 5, 0], [4, 7, 1, 2, 6, 3, 5, 0]],
+        [[1, 5, 2, 6, 7, 3, 4, 0], [1, 2, 6, 3, 7, 5, 0, 4], [0, 1, 3, 7, 4, 2, 6, 5], [4, 2, 5, 7, 3, 6, 0, 1]],
+        [[2, 5, 1, 7, 4, 0, 3, 6], [5, 4, 0, 3, 7, 6, 1, 2], [4, 0, 5, 7, 6, 1, 2, 3], [0, 1, 4, 6, 5, 2, 3, 7]],
+        [[7, 5, 6, 2, 1, 4, 3, 0], [5, 7, 3, 2, 1, 0, 6, 4], [6, 1, 3, 4, 5, 7, 0, 2], [0, 3, 2, 4, 6, 1, 5, 7]],
     ],
     [
-        [[5, 6, 4, 0, 3, 1, 7, 2], [2, 6, 0, 3, 4, 5, 1, 7], [7, 5, 3, 1, 4, 0, 2, 6], [0, 1, 7, 3, 2, 4, 6, 5]],
-        [[4, 2, 6, 1, 5, 7, 0, 3], [7, 2, 6, 5, 0, 4, 3, 1], [3, 7, 0, 6, 1, 2, 5, 4], [6, 3, 2, 5, 4, 1, 0, 7]],
-        [[3, 5, 1, 7, 6, 0, 4, 2], [2, 4, 5, 1, 7, 3, 6, 0], [5, 3, 4, 7, 1, 0, 6, 2], [2, 0, 1, 5, 7, 6, 3, 4]],
-        [[0, 4, 7, 6, 2, 1, 3, 5], [6, 0, 1, 2, 3, 5, 7, 4], [5, 0, 1, 2, 4, 7, 6, 3], [3, 6, 4, 5, 2, 7, 1, 0]],
-        [[1, 6, 2, 3, 5, 7, 4, 0], [0, 4, 7, 3, 5, 2, 1, 6], [1, 7, 2, 4, 3, 6, 5, 0], [0, 1, 7, 3, 6, 2, 4, 5]],
-        [[0, 1, 6, 7, 3, 5, 4, 2], [6, 0, 5, 3, 7, 4, 2, 1], [4, 2, 5, 7, 3, 6, 0, 1], [5, 4, 3, 6, 7, 2, 1, 0]],
-        [[2, 5, 1, 4, 7, 0, 3, 6], [2, 3, 0, 4, 7, 1, 6, 5], [1, 0, 3, 7, 6, 5, 2, 4], [6, 2, 4, 7, 5, 3, 0, 1]],
-        [[4, 1, 5, 2, 0, 6, 7, 3], [4, 6, 2, 0, 1, 3, 5, 7], [7, 1, 0, 6, 4, 2, 5, 3], [1, 7, 3, 4, 5, 0, 2, 6]],
+        [[5, 6, 0, 2, 1, 3, 4, 7], [1, 5, 6, 3, 2, 4, 0, 7], [2, 0, 3, 7, 4, 5, 1, 6], [7, 2, 1, 6, 4, 0, 5, 3]],
+        [[5, 1, 4, 7, 3, 6, 2, 0], [3, 0, 5, 4, 7, 6, 2, 1], [1, 5, 2, 6, 7, 0, 4, 3], [7, 3, 5, 4, 2, 0, 1, 6]],
+        [[2, 3, 0, 7, 1, 4, 6, 5], [5, 0, 3, 1, 7, 2, 6, 4], [0, 2, 7, 5, 4, 6, 3, 1], [3, 4, 6, 2, 5, 1, 7, 0]],
+        [[4, 7, 6, 2, 5, 3, 0, 1], [7, 4, 1, 6, 2, 5, 0, 3], [4, 0, 7, 2, 3, 1, 5, 6], [0, 7, 1, 3, 2, 6, 4, 5]],
+        [[6, 4, 7, 2, 5, 1, 0, 3], [5, 6, 3, 7, 2, 1, 4, 0], [0, 1, 4, 5, 3, 7, 6, 2], [1, 5, 2, 3, 6, 7, 4, 0]],
+        [[5, 3, 2, 7, 6, 4, 0, 1], [0, 1, 6, 5, 7, 2, 3, 4], [1, 0, 4, 7, 3, 6, 2, 5], [2, 1, 4, 3, 7, 5, 6, 0]],
+        [[4, 6, 0, 3, 7, 1, 5, 2], [6, 1, 0, 4, 3, 2, 7, 5], [0, 6, 3, 4, 7, 5, 2, 1], [1, 3, 5, 7, 4, 6, 0, 2]],
+        [[2, 5, 1, 6, 7, 0, 3, 4], [4, 2, 0, 5, 6, 3, 1, 7], [3, 0, 5, 7, 6, 2, 1, 4], [6, 3, 1, 7, 5, 0, 4, 2]],
     ],
 ]
 
@@ -180,18 +180,21 @@
 
     pl.semaphore_wait(barrier, members - 1 + jnp.where(early, ring - 1, windows - 1))
 
-    late_rows = sorted(range(ring), key=lambda row: min(row, ring - row), reverse=True)
-    late_first = [(row, half, core) for row in late_rows for half in range(2) for core in range(2)]
-    for row, half, core in late_first:
-        peer = (half * ring + row) * 2 + core
+
+    mixed_rows = [row % ring for row in (4, 1, 3, 7, 5, 2, 6, 0)][-ring:]
+    mixed_rows = sorted(set(mixed_rows), key=mixed_rows.index)
+    mixed = [(row, half, core) for core in range(2) for half in (1, 0) for row in mixed_rows]
+    for row_step, half_step, core_step in mixed:
+        if row_step + half_step + core_step == 0:
+            continue
+        row = lax.rem(my_row + row_step, ring)
+        peer = (lax.rem(my_half + half_step, 2) * ring + row) * 2 + lax.rem(my_core + core_step, 2)
         gap = wrap(row - my_row, ring)
         number = jnp.maximum(jnp.minimum(gap, ring - gap) - 1, 0)
 
-        @pl.when(peer != me)
-        def _():
-            remote(
-                outgoing.at[peer], incoming.at[me], tile_send, tile_recv.at[number], ctx=peer
-            ).start()
+        remote(
+            outgoing.at[peer], incoming.at[me], tile_send, tile_recv.at[number], ctx=peer
+        ).start()
 
     @pl.when(jnp.logical_not(early))
     def _():

time: 36.4 us -> 36.1 us (level)
  the two profiles are of different devices: /device:TPU:1 before, /device:TPU:22 now
where the time goes in v5:
time: 36.1 us; the launch traced here: 35.9 us
  Pallas kernels  35.2 us (98%)
  local copies, waits for them, and re-layouts  0.66 us (2%)
    pallas_call x1, Pallas kernels, per_device(): pl.pallas_call(functools.partial(kernel, members, windows), out_shape=plt...  35.2 us

profile of v5, /device:TPU:22, one launch (start us, length us, event | category | flops | bytes accessed | tf_op | source)
XLA Modules:
  0.0 35.9 jit_solution(12885583665444907959)
XLA Ops:
  0.0 35.2 %shard_map.91 = f32[128,256]{1,0:T(8,128)S(1)} custom-call(bf16[1,128,256]{2,1,0:T(8,128)(2,1)} %out_grad.1, bf16[1,128,256]{2,1,0:T(8,128)(2,1)} %gate_out.1, bf16[1,128,256]{2,1,0:T(8,128)(2,1)} %gate_in.1, bf16[1,128,256]{2,1,0:T(8,128)(2,1)} %values.1, s32[1,4]{1,0:T(1,128)} %doc_tiles.1, bf16[128,256]{1,0:T(8,128)(2,1)} %constant.8.clone.fwd_high, ...), custom_call_target="tpu_custom_call" | custom-call | tf_op jit(solution)/shard_map/pallas_call | solution.py:330
  35.2 0.7 %copy.11 = f32[128,256]{1,0:T(8,128)} copy(f32[128,256]{1,0:T(8,128)S(1)} %shard_map.91) | data formatting | bytes 262144

commit v6 on v5

--- a/solution.py
+++ b/solution.py
@@ -292,12 +292,12 @@
 
                 @pl.when(own)
                 def _():
-                    pltpu.make_async_copy(total.at[slot], landing.at[me], last_recv).start()
+                    pltpu.make_async_copy(total.at[slot], landing.at[me], last_recv.at[my_half]).start()
 
                 @pl.when(jnp.logical_not(own))
                 def _():
                     remote(
-                        total.at[slot], landing.at[me], last_send, last_recv, ctx=lag, dp=reader
+                        total.at[slot], landing.at[me], last_send, last_recv.at[my_half], ctx=lag, dp=reader
                     ).start()
 
     for slot in (lead, 1 - lead):
@@ -308,8 +308,13 @@
         spread(lead, [depth])
         spread(1 - lead, [depth])
 
-    wait_bytes(landing, last_recv)
-    out[...] = landing[...].reshape(channels, TILE).T
+    half = members // 2
+    for place in range(2):
+        blocks = pl.ds(place * half, half)
+        wait_bytes(landing.at[blocks], last_recv.at[place])
+        out[:, place * half * ROWS : (place + 1) * half * ROWS] = (
+            landing[blocks].reshape(half * ROWS, TILE).T
+        )
 
     wait_bytes(outgoing.at[pl.ds(0, members - 1)], tile_send)
     wait_bytes(lags.at[pl.ds(0, members - 2)], lag_send)
@@ -355,7 +360,7 @@
             pltpu.SemaphoreType.DMA,
             pltpu.SemaphoreType.DMA((2,)),
             pltpu.SemaphoreType.DMA,
-            pltpu.SemaphoreType.DMA,
+            pltpu.SemaphoreType.DMA((2,)),
             pltpu.SemaphoreType.REGULAR,
         ],
         compiler_params=pltpu.CompilerParams(

time: 36.1 us -> 36.2 us (level)
  no operation moved by 1% of the time
where the time goes in v6:
time: 36.2 us; the launch traced here: 36 us
  Pallas kernels  35.3 us (98%)
  local copies, waits for them, and re-layouts  0.66 us (2%)
    pallas_call x1, Pallas kernels, per_device(): pl.pallas_call(functools.partial(kernel, members, windows), out_shape=plt...  35.3 us

profile of v6, /device:TPU:22, one launch (start us, length us, event | category | flops | bytes accessed | tf_op | source)
XLA Modules:
  0.0 36.0 jit_solution(5149317167262353635)
XLA Ops:
  0.0 35.3 %shard_map.91 = f32[128,256]{1,0:T(8,128)S(1)} custom-call(bf16[1,128,256]{2,1,0:T(8,128)(2,1)} %out_grad.1, bf16[1,128,256]{2,1,0:T(8,128)(2,1)} %gate_out.1, bf16[1,128,256]{2,1,0:T(8,128)(2,1)} %gate_in.1, bf16[1,128,256]{2,1,0:T(8,128)(2,1)} %values.1, s32[1,4]{1,0:T(1,128)} %doc_tiles.1, bf16[128,256]{1,0:T(8,128)(2,1)} %constant.8.clone.fwd_high, ...), custom_call_target="tpu_custom_call" | custom-call | tf_op jit(solution)/shard_map/pallas_call | solution.py:335
  35.4 0.7 %copy.11 = f32[128,256]{1,0:T(8,128)} copy(f32[128,256]{1,0:T(8,128)S(1)} %shard_map.91) | data formatting | bytes 262144

commit v7 on v5

--- a/solution.py
+++ b/solution.py
@@ -183,7 +183,7 @@
 
     mixed_rows = [row % ring for row in (4, 1, 3, 7, 5, 2, 6, 0)][-ring:]
     mixed_rows = sorted(set(mixed_rows), key=mixed_rows.index)
-    mixed = [(row, half, core) for core in range(2) for half in (1, 0) for row in mixed_rows]
+    mixed = [(row, half, core) for half in (1, 0) for core in (1, 0) for row in mixed_rows]
     for row_step, half_step, core_step in mixed:
         if row_step + half_step + core_step == 0:
             continue

time: 36.1 us -> 36 us (level)
  the two profiles are of different devices: /device:TPU:22 before, /device:TPU:1 now
where the time goes in v7:
time: 36 us; the launch traced here: 35.6 us
  Pallas kernels  34.9 us (97%)
  local copies, waits for them, and re-layouts  0.66 us (2%)
    pallas_call x1, Pallas kernels, per_device(): pl.pallas_call(functools.partial(kernel, members, windows), out_shape=plt...  34.9 us

profile of v7, /device:TPU:1, one launch (start us, length us, event | category | flops | bytes accessed | tf_op | source)
XLA Modules:
  0.0 35.6 jit_solution(8577915153360524761)
XLA Ops:
  0.0 34.9 %shard_map.91 = f32[128,256]{1,0:T(8,128)S(1)} custom-call(bf16[1,128,256]{2,1,0:T(8,128)(2,1)} %out_grad.1, bf16[1,128,256]{2,1,0:T(8,128)(2,1)} %gate_out.1, bf16[1,128,256]{2,1,0:T(8,128)(2,1)} %gate_in.1, bf16[1,128,256]{2,1,0:T(8,128)(2,1)} %values.1, s32[1,4]{1,0:T(1,128)} %doc_tiles.1, bf16[128,256]{1,0:T(8,128)(2,1)} %constant.8.clone.fwd_high, ...), custom_call_target="tpu_custom_call" | custom-call | tf_op jit(solution)/shard_map/pallas_call | solution.py:330
  34.9 0.7 %copy.11 = f32[128,256]{1,0:T(8,128)} copy(f32[128,256]{1,0:T(8,128)S(1)} %shard_map.91) | data formatting | bytes 262144
